TPU v7x, 128 devices: a whole 4x4x4 slice. The times are simulated.
128 devices in a mesh: arc: 8 (over x_hi, z), col: 16 (over x_lo, y, core).
Axes of the slice: x: 4 (x_hi: 2, x_lo: 2; x = x_hi * 2 + x_lo), y: 4, z: 4, core: 2. Of those that a mesh axis runs over, the one named last changes fastest.
Arguments:
- local_obs: float32 [1024, 320, 128], P(('arc', 'col')), may hold values from -6 to 6
- global_obs: float32 [1024, 320, 512], P('arc', None, 'col'), may hold values from -0.75 to 0.75
- row_counts: int32 [1024], P('arc'), may hold values from 160 to 320, as said below
- owner_map: int32 [1024], P(('arc', 'col')), may hold values from 0 to 255, as said below
- prior_factor: float32 [256, 512, 512], P(('arc', 'col')), as said below
Outputs:
- updated_factor: float32 [256, 512, 512], P(('arc', 'col'))
Inputs may be any that keep to these rules, and one draw needn't show every extreme that they name: `row_counts`: between 160 and 320; some arc has exactly 320 rows and another exactly 160. `owner_map`: the slice of arc k lies on a device with the same col index as the device that holds local_obs[k]; slice s lies on device s // 2 in arc+col order; from the 8 arcs of one device at most 2 have slices on devices of one arc index, and exactly 2 on one of them; in each col index one device receives 2 arcs from every device of that col index. `prior_factor`: each slice's factor is upper triangular with a positive diagonal.
All inputs are finite; a program needn't handle non-finite values.
Results may differ from a plain program's by a relative error of at most 0.0003.
Values sent between devices are 32-bit elements; how exact they have to be, the bound alone decides.
No kernel may reach another device: no remote copies, remote signals or barrier semaphores. Data moves between devices by JAX's collectives and lax.ppermute only.
A program may use at most 128 MiB of HBM per device.

v0:
```python
import functools

import jax
import jax.numpy as jnp
from jax import lax
from jax.experimental import pallas as pl
from jax.experimental.pallas import tpu as pltpu
from jax.sharding import PartitionSpec as P

SLICE_DEV = 2
HI = lax.Precision.HIGHEST
F32 = jnp.float32
BF16 = jnp.bfloat16
NN = (((1,), (0,)), ((), ()))
NT = (((1,), (1,)), ((), ()))
TN = (((0,), (0,)), ((), ()))
VMEM_LIMIT = 60 * 1024 * 1024


def dot(a, b, dims, precision=None):
    return lax.dot_general(a, b, dims, precision=precision, preferred_element_type=F32)


def split2(x):
    high = x.astype(BF16)
    return high, (x - high.astype(F32)).astype(BF16)


def dot3(a, b, dims):
    ah, al = a
    bh, bl = b
    ka, kb = dims[0][0][0], dims[0][1][0]
    left = jnp.concatenate([ah, ah, al], axis=ka)
    return dot(left, jnp.concatenate([bh, bl, bh], axis=kb), dims)


def split3(x):
    high = x.astype(BF16).astype(F32)
    rest = x - high
    mid = rest.astype(BF16).astype(F32)
    return high, mid, rest - mid


def outer6(left, right):
    lh, lm, ll = split3(left)
    rh, rm, rl = split3(right)
    a = jnp.concatenate([lh, lh, lm, lh, ll, lm], axis=0).astype(BF16)
    b = jnp.concatenate([rh, rm, rh, rl, rh, rm], axis=0).astype(BF16)
    return dot(a, b, TN)


def outer3(left, right):
    lh, lm, _ = split3(left)
    rh, rm, _ = split3(right)
    a = jnp.concatenate([lh, lh, left - lh], axis=0).astype(BF16)
    b = jnp.concatenate([rh, right - rh, rh], axis=0).astype(BF16)
    return dot(a, b, TN)


def row_of(x, i):
    return jnp.broadcast_to(x[:, i : i + 1, :], x.shape)


def lane_of(x, i):
    return jnp.broadcast_to(x[:, :, i : i + 1], x.shape)


def panel_rows(p):
    return pl.ds(pl.multiple_of(8 * p, 8), 8)


def places(x, p):
    lane = lax.broadcasted_iota(jnp.int32, x.shape, 2) - 8 * p
    return lane, lax.broadcasted_iota(jnp.int32, x.shape, 1)


def columns_of(x, p):
    turned = pltpu.roll(x, lax.rem(128 - 8 * p, 128), 2)
    return [lane_of(turned, l) for l in range(8)]


def batch_panel(x, following, p):
    lane, sub = places(x, p)
    inside = (lane >= 0) & (lane < 8)
    c = columns_of(x, p)
    n = columns_of(following, p)
    place = jnp.where(inside, (lane == sub).astype(F32), x)
    following = jnp.where(inside, 0.0, following)
    pivots = x
    for i in range(8):
        d = row_of(c[i], i)
        inv = pl.reciprocal(d, approx=True)
        pivots = jnp.where(sub == i, d, pivots)
        below = jnp.where(sub > i, c[i], 0.0)
        below_n = n[i]
        for l in range(i + 1, 8):
            r = row_of(c[l], i)
            c[l] = c[l] - (below * r) * inv
            n[l] = n[l] - (below_n * r) * inv
        below = below * inv
        r = row_of(place, i)
        place = place - below * r
        following = following - (below_n * inv) * r
    scale = lax.rsqrt(pivots)
    return place * scale, following


def cholesky_batch(a_ref):
    count = a_ref.shape[0]

    def step(p, carry):
        left, right, x = carry
        a = a_ref[...]
        at_lane, at_row = places(a, p)
        t = jnp.stack([outer6(left[b], right[b]) for b in range(count)], axis=0)
        cleared = (at_lane < 0) & (at_lane >= -8) & (at_row >= 8 * p + 8)
        a_ref[...] = jnp.where(cleared, 0.0, a) - t
        following = a_ref[:, panel_rows(jnp.minimum(p + 1, 15)), :]
        place, following = batch_panel(x, following, p)
        lane, sub = places(x, p)
        a_ref[:, panel_rows(p), :] = place
        return jnp.where(lane >= 16, place, 0.0), place, following

    first = a_ref[:, :8, :]
    lax.fori_loop(0, 16, step, (jnp.zeros_like(first), jnp.zeros_like(first), first))


def columns_at(x, p):
    return [lane_of(x, 8 * p + l) for l in range(8)]


def cholesky_panel(x, c, following, p):
    lane, sub = places(x, p)
    inside = (lane >= 0) & (lane < 8)
    c = list(c)
    place = jnp.where(inside, (lane == sub).astype(F32), x)
    n = ahead = None
    if following is not None:
        n = columns_at(following, p)
        ahead = columns_at(following, p + 1)
        following = jnp.where(inside, 0.0, following)
    upper = x
    pivots = x
    for i in range(8):
        d = row_of(c[i], i)
        inv = pl.reciprocal(d, approx=True)
        pivots = jnp.where(sub == i, d, pivots)
        below = jnp.where(sub > i, c[i], 0.0)
        for l in range(i + 1, 8):
            r = row_of(c[l], i) * inv
            c[l] = c[l] - below * r
            if n is not None:
                n[l] = n[l] - n[i] * r
        r = row_of(place, i) * inv
        place = place - below * r
        if n is not None:
            following = following - n[i] * r
            less = n[i] * inv
            ahead = [ahead[l] - less * row_of(n[i], l) for l in range(8)]
        upper = upper - below * (row_of(upper, i) * inv)
    scale = lax.rsqrt(pivots)
    return upper * scale, place * scale, following, ahead


def cholesky_blocks(a_ref, store_upper):
    count = a_ref.shape[0]
    rows = [a_ref[:, 8 * q : 8 * q + 8, :] for q in range(16)]
    c = columns_at(rows[0], 0)
    for p in range(16):
        following = rows[p + 1] if p < 15 else None
        upper, place, following, c = cholesky_panel(rows[p], c, following, p)
        lane, sub = places(place, p)
        inside = (lane >= 0) & (lane < 8)
        a_ref[:, 8 * p : 8 * p + 8, :] = place
        if store_upper is not None:
            store_upper(p, jnp.where(lane >= sub, upper, 0.0))
        if p < 15:
            rows[p + 1] = following
        if p < 14:
            left = jnp.where(lane >= 16, place, 0.0)
            t = [outer3(left[b], place[b]) for b in range(count)]
            for q in range(p + 2, 16):
                part = jnp.stack([v[8 * q : 8 * q + 8] for v in t], axis=0)
                rows[q] = jnp.where(inside, 0.0, rows[q]) - part


def inverse_panel(a_ref, sign_ref, p):
    x = a_ref[:, panel_rows(p), :]
    lane, sub = places(x, p)
    c = columns_of(x, p)
    place = jnp.where((lane >= 0) & (lane < 8), (lane == sub).astype(F32), x)
    signs = sign_ref[...]
    for i in range(8):
        pv = row_of(c[i], i)
        s = jnp.where(pv >= 0.0, -1.0, 1.0)
        signs = jnp.where(lane == i, s, signs)
        inv = pl.reciprocal(pv - s, approx=True)
        lm = jnp.where(sub == i, 1.0 - inv, c[i] * inv)
        for l in range(i + 1, 8):
            c[l] = c[l] - lm * row_of(c[l], i)
        place = place - lm * row_of(place, i)
    sign_ref[...] = signs
    a = a_ref[...]
    at_lane, at_row = places(a, p)
    wide = jnp.concatenate([place] * 16, axis=1)
    factor = jnp.where((at_row >= 8 * p) & (at_row < 8 * p + 8), wide, 0.0)
    t = jnp.stack([dot(a[b], factor[b], NN, HI) for b in range(x.shape[0])], axis=0)
    a_ref[...] = jnp.where((at_lane >= 0) & (at_lane < 8), 0.0, a) - t
    a_ref[:, panel_rows(p), :] = place


def layout_kernel(x_ref, o_ref, x_buf, o_buf, in_sems, out_sems):
    rows, cols, arcs = x_ref.shape
    blocks = cols // 8
    arriving = []
    for b in range(blocks):
        copy = pltpu.make_async_copy(x_ref.at[:, 8 * b : 8 * b + 8, :], x_buf.at[b], in_sems.at[b])
        copy.start()
        arriving.append(copy)
    leaving = []

    def put(row, tiles):
        o_buf[:, row : row + 8, :] = jnp.transpose(tiles, (1, 0, 2))
        where = slice(row, row + 8)
        copy = pltpu.make_async_copy(o_buf.at[:, where, :], o_ref.at[:, where, :], out_sems.at[len(leaving)])
        copy.start()
        leaving.append(copy)

    ends = []
    for b in range(blocks):
        arriving[b].wait()
        for tile in range(2):
            v = jnp.transpose(x_buf[b, 128 * tile : 128 * tile + 128], (1, 0, 2))
            put(tile * cols + 8 * b, jnp.stack([v[c].T for c in range(8)], axis=0))
        ends.append(jnp.transpose(x_buf[b, 256:], (1, 0, 2)))
        if b % 2:
            both = jnp.concatenate(ends, axis=1)
            put(2 * cols + 4 * (b - 1), jnp.stack([both[c].T for c in range(8)], axis=0))
            ends = []
    for copy in leaving:
        copy.wait()


def layout(x):
    rows, cols, arcs = x.shape
    packed = 2 * cols + cols // 2
    hbm = pl.BlockSpec(memory_space=pltpu.HBM)
    return pl.pallas_call(
        layout_kernel,
        out_shape=jax.ShapeDtypeStruct((arcs, packed, 128), F32),
        in_specs=[hbm],
        out_specs=hbm,
        scratch_shapes=[
            pltpu.VMEM((cols // 8, rows, 8, arcs), F32),
            pltpu.VMEM((arcs, packed, 128), F32),
            pltpu.SemaphoreType.DMA((cols // 8,)),
            pltpu.SemaphoreType.DMA((packed // 8,)),
        ],
        compiler_params=pltpu.CompilerParams(vmem_limit_bytes=VMEM_LIMIT),
    )(x)


def local_kernel(counts_ref, l_ref, prior_ref, z_ref, info_ref, a_ref, q_ref, sign_ref):
    arcs, rows, loc = l_ref.shape
    place = lax.broadcasted_iota(jnp.int32, (rows, loc), 0)
    for b in range(arcs):
        masked = jnp.where(place < counts_ref[b], l_ref[b], 0.0)
        q_ref[b] = masked
        a_ref[b] = dot(masked, masked, TN, HI)
    cholesky_batch(a_ref)
    r = lax.broadcasted_iota(jnp.int32, (loc, loc), 0)
    l = lax.broadcasted_iota(jnp.int32, (loc, loc), 1)
    for b in range(arcs):
        basis = dot(q_ref[b], jnp.where(l <= r, a_ref[b], 0.0), NT, HI)
        q_ref[b] = basis
        a_ref[b] = basis[:loc]
    sign_ref[...] = jnp.zeros_like(sign_ref)

    def invert(p, carry):
        inverse_panel(a_ref, sign_ref, p)
        return carry

    lax.fori_loop(0, loc // 8, invert, 0)
    rest = rows - loc
    unit = (place == lax.broadcasted_iota(jnp.int32, (rows, loc), 1)).astype(F32)
    r2 = lax.broadcasted_iota(jnp.int32, (rest, rows), 0)
    l2 = lax.broadcasted_iota(jnp.int32, (rest, rows), 1)
    for b in range(arcs):
        q = q_ref[b]
        n = dot(q[loc:], a_ref[b], NN, HI)
        v = q * sign_ref[b][0:1] - unit
        keep = (l2 == r2 + loc) & (l2 < counts_ref[b])
        z = dot(n, v, NT, HI) + keep.astype(F32)
        zh, zl = split2(jnp.concatenate([z, z[:, 256:]], axis=1))
        z_ref[b, 0] = zh
        z_ref[b, 1] = zl
    half = prior_ref.shape[1] // 2
    for s in range(prior_ref.shape[0]):
        top = prior_ref[s, :half, :]
        low = prior_ref[s, :, half:]
        info_ref[s, :half, :] = dot(top[:, :half], top, TN, HI)
        info_ref[s, half:, half:] = dot(low, low, TN, HI)
        info_ref[s, half:, :half] = jnp.zeros((half, half), F32)


def local_part(counts, local_obs, prior):
    arcs, rows, loc = local_obs.shape
    vmem = pl.BlockSpec(memory_space=pltpu.VMEM)
    return pl.pallas_call(
        local_kernel,
        out_shape=(
            jax.ShapeDtypeStruct((arcs, 2, rows - loc, 384), BF16),
            jax.ShapeDtypeStruct(prior.shape, F32),
        ),
        in_specs=[pl.BlockSpec(memory_space=pltpu.SMEM), vmem, vmem],
        out_specs=(vmem, vmem),
        scratch_shapes=[
            pltpu.VMEM((arcs, loc, loc), F32),
            pltpu.VMEM((arcs, rows, loc), F32),
            pltpu.VMEM((arcs, 8, loc), F32),
        ],
        compiler_params=pltpu.CompilerParams(vmem_limit_bytes=VMEM_LIMIT),
    )(counts, local_obs, prior)


def eliminate_kernel(
    dest_ref, slot_ref, label_ref, g_hbm, z_hbm, o_ref, g_buf, z_buf, main_ref, tail_ref, g_sems, z_sems, sems, tail_sem
):
    arcs, sources, packed, _ = g_buf.shape
    part = packed * 2 // 5
    width = sources * part

    def columns(a):
        return pltpu.make_async_copy(g_hbm.at[:, a], g_buf.at[a], g_sems.at[a])

    def weights(a):
        return pltpu.make_async_copy(z_hbm.at[a], z_buf.at[a], z_sems.at[a])

    for a in range(arcs):
        columns(a).start()
        weights(a).start()
    tail_ref[...] = jnp.zeros_like(tail_ref)
    tail_ref[:, width:, :] = jnp.full((tail_ref.shape[0], 8, 128), -1.0, F32)

    def reduced(a):
        g = [g_buf[a, :, i * part : (i + 1) * part, :].reshape(width, 128) for i in range(2)]
        t = g_buf[a, :, 2 * part :, :].reshape(width // 16, 8, 128)
        first = lax.broadcasted_iota(jnp.int32, t.shape, 2) < 64
        ends = jnp.stack([jnp.where(own, t, 0.0) for own in (first, ~first)], axis=1).reshape(width, 128)
        zh, zl = [jnp.concatenate([z_buf[a, i], jnp.zeros((64, 384), BF16)], axis=0) for i in range(2)]
        return dot3(split2(jnp.concatenate([*g, ends], axis=1)), (zh, zl), NT)

    def pair(i, carry):
        both = (2 * i, 2 * i + 1)
        for a in both:
            columns(a).wait()
            weights(a).wait()
        results = [reduced(a) for a in both]
        for a, r in zip(both, results):
            slot = slot_ref[a]
            dest = dest_ref[a]
            main_ref[a] = r[:, :128]
            rows = pl.ds(pl.multiple_of(width * slot, 8), width)
            pltpu.make_async_copy(main_ref.at[a], o_ref.at[dest, rows, :], sems.at[a]).start()
            tail_ref[dest, :width, :] += pltpu.roll(r[:, 128:], 64 * slot, 1)
            labels = tail_ref[dest, width:, :]
            at = lax.broadcasted_iota(jnp.int32, labels.shape, 0)
            tail_ref[dest, width:, :] = jnp.where(at == slot, label_ref[a].astype(F32), labels)
        return carry

    lax.fori_loop(0, arcs // 2, pair, 0)
    ends_copy = pltpu.make_async_copy(tail_ref, o_ref.at[:, 2 * width :, :], tail_sem)
    ends_copy.start()
    for a in range(arcs):
        pltpu.make_async_copy(main_ref.at[a], o_ref.at[0, :width, :], sems.at[a]).wait()
    ends_copy.wait()


def eliminate(dest, slot, label, g, z, groups):
    sources, arcs, packed, _ = g.shape
    width = sources * packed * 2 // 5
    smem = pl.BlockSpec(memory_space=pltpu.SMEM)
    hbm = pl.BlockSpec(memory_space=pltpu.HBM)
    return pl.pallas_call(
        eliminate_kernel,
        out_shape=jax.ShapeDtypeStruct((groups, 3 * width + 8, 128), F32),
        in_specs=[smem, smem, smem, hbm, hbm],
        out_specs=hbm,
        scratch_shapes=[
            pltpu.VMEM((arcs, sources, packed, 128), F32),
            pltpu.VMEM(z.shape, BF16),
            pltpu.VMEM((arcs, width, 128), F32),
            pltpu.VMEM((groups, width + 8, 128), F32),
            pltpu.SemaphoreType.DMA((arcs,)),
            pltpu.SemaphoreType.DMA((arcs,)),
            pltpu.SemaphoreType.DMA((arcs,)),
            pltpu.SemaphoreType.DMA,
        ],
        compiler_params=pltpu.CompilerParams(vmem_limit_bytes=VMEM_LIMIT),
    )(dest, slot, label, g, z)


def factor_kernel(x_hbm, prior_ref, out_hbm, list_ref, x_buf, info_ref, out_ref, a_ref, sems, prior_sem, out_sems):
    slices, width, _ = info_ref.shape
    groups = x_buf.shape[0] - 1
    half = width // 2

    def rows_of(n):
        return pltpu.make_async_copy(x_hbm.at[n], x_buf.at[n], sems.at[n])

    start = pltpu.make_async_copy(prior_ref, info_ref, prior_sem)
    start.start()
    for n in range(groups):
        rows_of(n).start()
    x_buf[groups] = jnp.zeros_like(x_buf[groups])
    start.wait()

    def listed(n, count):
        rows_of(n).wait()
        labels = x_buf[n, 3 * width :, :]
        for slot in range(2):
            label = labels[slot, 0].astype(jnp.int32)
            list_ref[0, count] = n
            list_ref[1, count] = slot
            list_ref[2, count] = label
            count = count + (label >= 0).astype(jnp.int32)
        return count

    count = lax.fori_loop(0, groups, listed, 0)
    list_ref[0, count] = groups
    list_ref[1, count] = 0
    list_ref[2, count] = 0

    def add(pair, carry):
        items = []
        for i in range(2):
            n, slot = list_ref[0, 2 * pair + i], list_ref[1, 2 * pair + i]
            main = x_buf[n, pl.ds(pl.multiple_of(slot * width, 8), width), :]
            tail = x_buf[n, 2 * width : 3 * width, :]
            own = lax.broadcasted_iota(jnp.int32, tail.shape, 1) // 64 == slot
            h, l = split2(jnp.concatenate([main, jnp.where(own, tail, 0.0)], axis=1))
            top = dot3((h[:half], l[:half]), (h, l), NT)
            items.append((list_ref[2, 2 * pair + i], top, dot3((h[half:], l[half:]), (h[half:], l[half:]), NT)))
        for label, top, low in items:
            info_ref[label, :half, :] += top
            info_ref[label, half:, half:] += low
        return carry

    lax.fori_loop(0, (count + 1) // 2, add, 0)
    r = lax.broadcasted_iota(jnp.int32, (128, 128), 0)
    l = lax.broadcasted_iota(jnp.int32, (128, 128), 1)
    leaving = []
    for k in range(width // 128):
        lo, hi = 128 * k, 128 * k + 128
        block = a_ref.at[k % 2]
        block[...] = info_ref[:, lo:hi, lo:hi]
        if k:
            out_ref[:, lo:hi, :lo] = jnp.zeros((slices, 128, lo), F32)

        def store(p, rows):
            out_ref[:, lo + 8 * p : lo + 8 * p + 8, lo:hi] = rows

        cholesky_blocks(block, store)
        inverses = [split2(jnp.where(l <= r, block[s], 0.0)) for s in range(slices)]
        right = [[None] * slices for _ in range(width // 128)]
        for j in range(k + 1, width // 128):
            for s in range(slices):
                u = dot3(inverses[s], split2(info_ref[s, lo:hi, 128 * j : 128 * j + 128]), NN)
                out_ref[s, lo:hi, 128 * j : 128 * j + 128] = u
                right[j][s] = split2(u)
            for i in range(k + 1, j + 1):
                for s in range(slices):
                    less = dot3(right[i][s], right[j][s], TN)
                    info_ref[s, 128 * i : 128 * i + 128, 128 * j : 128 * j + 128] -= less
        copy = pltpu.make_async_copy(out_ref.at[:, lo:hi, :], out_hbm.at[:, lo:hi, :], out_sems.at[k])
        copy.start()
        leaving.append(copy)
    for copy in leaving:
        copy.wait()


def factor(arrived, prior_gram):
    slices, width, _ = prior_gram.shape
    hbm = pl.BlockSpec(memory_space=pltpu.HBM)
    return pl.pallas_call(
        factor_kernel,
        out_shape=jax.ShapeDtypeStruct(prior_gram.shape, F32),
        in_specs=[hbm, pl.BlockSpec(memory_space=pl.ANY)],
        out_specs=hbm,
        scratch_shapes=[
            pltpu.SMEM((3, 2 * arrived.shape[0] + 1), jnp.int32),
            pltpu.VMEM((arrived.shape[0] + 1, *arrived.shape[1:]), F32),
            pltpu.VMEM((slices, width, width), F32),
            pltpu.VMEM((slices, width, width), F32),
            pltpu.VMEM((2, slices, 128, 128), F32),
            pltpu.SemaphoreType.DMA((arrived.shape[0],)),
            pltpu.SemaphoreType.DMA,
            pltpu.SemaphoreType.DMA((width // 128,)),
        ],
        compiler_params=pltpu.CompilerParams(vmem_limit_bytes=VMEM_LIMIT),
    )(arrived, prior_gram)


def per_device(local_obs, global_obs, row_counts, owner_map, prior_factor):
    arc_dev = local_obs.shape[0]
    arc_groups = lax.axis_size("arc")
    col_groups = lax.axis_size("col")
    counts = lax.dynamic_slice_in_dim(row_counts, lax.axis_index("col") * arc_dev, arc_dev)
    packed = layout(jnp.transpose(global_obs, (1, 2, 0)))
    columns = lax.all_to_all(packed, "col", split_axis=0, concat_axis=0, tiled=True)
    columns = columns.reshape(col_groups, arc_dev, *packed.shape[1:])
    order = jnp.arange(arc_dev, dtype=jnp.int32)
    dest = owner_map // SLICE_DEV // col_groups
    earlier = (dest[None, :] == dest[:, None]) & (order[None, :] < order[:, None])
    slot = jnp.sum(earlier.astype(jnp.int32), axis=1)
    z, prior_gram = local_part(counts, local_obs, prior_factor)
    kept = eliminate(dest, slot, owner_map % SLICE_DEV, columns, z, arc_groups)
    arrived = lax.all_to_all(kept, "arc", split_axis=0, concat_axis=0, tiled=True)
    return factor(arrived, prior_gram)


def solution(mesh):
    placed = (
        P(("arc", "col"), None, None),
        P("arc", None, "col"),
        P("arc"),
        P(("arc", "col")),
        P(("arc", "col"), None, None),
    )
    return jax.shard_map(
        per_device,
        mesh=mesh,
        in_specs=placed,
        out_specs=P(("arc", "col"), None, None),
        check_vma=False,
    )
```

profile of v0, /device:TPU:24, one launch (start us, length us, event | category | flops | bytes accessed | tf_op | source)
XLA Modules:
  0.0 203.7 jit_solution(3070889630601297263)
XLA Ops:
  0.0 4.5 %shard_map.55 = f32[128,80,128]{2,1,0:T(8,128)} custom-call(f32[320,32,128]{2,1,0:T(8,128)} %bitcast.2), custom_call_target="tpu_custom_call" | custom-call | tf_op jit(solution)/shard_map/pallas_call | solution.py:248
  4.5 0.0 copy-start.1
  4.5 0.0 copy-start.2
  4.5 5.6 %all-to-all-start = ((f32[128,80,128]{2,1,0:T(8,128)}), f32[128,80,128]{2,1,0:T(8,128)}, u32[]{:S(2)}, u32[]{:S(2)}) async-start(f32[128,80,128]{2,1,0:T(8,128)} %shard_map.55), calls=%async_computation | async-start | bytes 10485760 | tf_op jit(solution)/shard_map/all_to_all | solution.py:510
  10.2 0.0 copy-done.1
  10.2 0.6 dynamic_slice.3.counts_ref
  10.8 39.8 %shard_map.56 = (bf16[8,2,192,384]{3,2,1,0:T(8,128)(2,1)}, f32[2,512,512]{2,1,0:T(8,128)}) custom-call(s32[8]{0:T(128)} %dynamic_slice.3.counts_ref, f32[8,320,128]{2,1,0:T(8,128)} %l_ref.1, f32[2,512,512]{2,1,0:T(8,128)} %prior_ref.1), custom_call_target="tpu_custom_call" | custom-call | tf_op jit(solution)/shard_map/pallas_call | solution.py:309
  50.5 0.0 copy-done.2
  50.5 0.5 and_select_fusion
  51.1 0.0 copy-start
  51.1 0.7 convert_reduce_fusion.slot_ref
  51.8 36.5 %all-to-all-done = f32[128,80,128]{2,1,0:T(8,128)} async-done(((f32[128,80,128]{2,1,0:T(8,128)}), f32[128,80,128]{2,1,0:T(8,128)}, u32[]{:S(2)}, u32[]{:S(2)}) %all-to-all-start) | async-done | bytes 5242912 | tf_op jit(solution)/shard_map/all_to_all | solution.py:510
  88.2 0.0 copy-done
  88.2 7.6 %shard_map.57 = f32[8,1544,128]{2,1,0:T(8,128)} custom-call(s32[8]{0:T(128)} %copy-done, s32[8]{0:T(128)} %convert_reduce_fusion.slot_ref, s32[8]{0:T(128)} %get-tuple-element.9.label_ref, f32[16,8,80,128]{3,2,1,0:T(8,128)} %bitcast.1.g_hbm, bf16[8,2,192,384]{3,2,1,0:T(8,128)(2,1)} %get-tuple-element.7.z_hbm), custom_call_target="tpu_custom_call" | custom-call | tf_op jit(solution)/shard_map/pallas_call | solution.py:384
  95.9 82.0 %all_to_all.10.x_hbm = f32[8,1544,128]{2,1,0:T(8,128)} all-to-all(f32[8,1544,128]{2,1,0:T(8,128)} %shard_map.57), channel_id=1, replica_groups=mesh['arc'=8,'col'=16] {'arc'}, dimensions={0} | all-to-all | bytes 12648448 | tf_op jit(solution)/shard_map/all_to_all | solution.py:518
  177.9 25.7 %shard_map.58 = f32[2,512,512]{2,1,0:T(8,128)} custom-call(f32[8,1544,128]{2,1,0:T(8,128)} %all_to_all.10.x_hbm, f32[2,512,512]{2,1,0:T(8,128)} %get-tuple-element.8.prior_ref), custom_call_target="tpu_custom_call" | custom-call | tf_op jit(solution)/shard_map/pallas_call | solution.py:485
Async XLA Ops:
  4.5 5.7 %copy-start.1 = (s32[128]{0:T(128)S(1)}, s32[128]{0:T(128)}, u32[]{:S(2)}) copy-start(s32[128]{0:T(128)} %param.7) | copy-start | bytes 1540
  4.5 46.0 %copy-start.2 = (s32[8]{0:T(128)S(1)}, s32[8]{0:T(128)}, u32[]{:S(2)}) copy-start(s32[8]{0:T(128)} %param.8) | copy-start | bytes 100
  4.5 83.7 %all-to-all-start = ((f32[128,80,128]{2,1,0:T(8,128)}), f32[128,80,128]{2,1,0:T(8,128)}, u32[]{:S(2)}, u32[]{:S(2)}) async-start(f32[128,80,128]{2,1,0:T(8,128)} %shard_map.55), calls=%async_computation | async-start | bytes 10485760 | tf_op jit(solution)/shard_map/all_to_all | solution.py:510
  51.1 37.2 %copy-start = (s32[8]{0:T(128)}, s32[8]{0:T(128)S(1)}, u32[]{:S(2)}) copy-start(s32[8]{0:T(128)S(1)} %get-tuple-element.10.dest_ref) | copy-start | bytes 100
where the time goes:
time: 206 us; the launch traced here: 204 us
  blocking collectives  82 us (40%)
  Pallas kernels  77.6 us (38%)
  waiting for transfers between devices  36.5 us (18%)
  starting transfers between devices  5.65 us (3%)
    all_to_all x1, blocking collectives, per_device(): lax.all_to_all(kept, 'arc', split_axis=0, concat_axis=0, tiled=True)  82 us
    pallas_call x1, Pallas kernels, local_part(): pl.pallas_call(local_kernel, out_shape=(jax.ShapeDtypeStruct((arcs, 2, ro...  39.8 us
    all_to_all x1, waiting for transfers between devices, per_device(): lax.all_to_all(packed, 'col', split_axis=0, concat_axis=0, tiled=True)  36.5 us
    pallas_call x1, Pallas kernels, factor(): pl.pallas_call(factor_kernel, out_shape=jax.ShapeDtypeStruct(prior_gram.s...  25.7 us
    pallas_call x1, Pallas kernels, eliminate(): pl.pallas_call(eliminate_kernel, out_shape=jax.ShapeDtypeStruct((groups,...  7.62 us
    all_to_all x1, starting transfers between devices, per_device(): lax.all_to_all(packed, 'col', split_axis=0, concat_axis=0, tiled=True)  5.65 us
    pallas_call x1, Pallas kernels, layout(): pl.pallas_call(layout_kernel, out_shape=jax.ShapeDtypeStruct((arcs, packe...  4.48 us
  transfers between devices with their start and end apart: 1, of which 1 were waited for; matrix products, arithmetic and copies ran while one was open for 1% of the time, Pallas kernels for 20%

commit v1 on v0

--- a/solution.py
+++ b/solution.py
@@ -400,24 +400,27 @@
     )(dest, slot, label, g, z)
 
 
-def factor_kernel(x_hbm, prior_ref, out_hbm, list_ref, x_buf, info_ref, out_ref, a_ref, sems, prior_sem, out_sems):
+def factor_kernel(
+    x_hbm, prior_ref, out_hbm, list_ref, label_buf, x_buf, info_ref, out_ref, a_ref, sems, label_sem, prior_sem, out_sems
+):
     slices, width, _ = info_ref.shape
     groups = x_buf.shape[0] - 1
     half = width // 2
 
     def rows_of(n):
-        return pltpu.make_async_copy(x_hbm.at[n], x_buf.at[n], sems.at[n])
-
+        return pltpu.make_async_copy(x_hbm.at[n, : 3 * width, :], x_buf.at[n], sems.at[n])
+
+    marks = pltpu.make_async_copy(x_hbm.at[:, 3 * width :, :], label_buf, label_sem)
+    marks.start()
     start = pltpu.make_async_copy(prior_ref, info_ref, prior_sem)
     start.start()
     for n in range(groups):
         rows_of(n).start()
     x_buf[groups] = jnp.zeros_like(x_buf[groups])
-    start.wait()
+    marks.wait()
 
     def listed(n, count):
-        rows_of(n).wait()
-        labels = x_buf[n, 3 * width :, :]
+        labels = label_buf[n]
         for slot in range(2):
             label = labels[slot, 0].astype(jnp.int32)
             list_ref[0, count] = n
@@ -430,9 +433,16 @@
     list_ref[0, count] = groups
     list_ref[1, count] = 0
     list_ref[2, count] = 0
-
-    def add(pair, carry):
+    start.wait()
+
+    def wait(n, carry):
+        rows_of(n).wait()
+        return carry
+
+    def add(pair, ready):
         items = []
+        needed = jnp.minimum(jnp.maximum(list_ref[0, 2 * pair], list_ref[0, 2 * pair + 1]) + 1, groups)
+        lax.fori_loop(ready, needed, wait, 0)
         for i in range(2):
             n, slot = list_ref[0, 2 * pair + i], list_ref[1, 2 * pair + i]
             main = x_buf[n, pl.ds(pl.multiple_of(slot * width, 8), width), :]
@@ -444,9 +454,10 @@
         for label, top, low in items:
             info_ref[label, :half, :] += top
             info_ref[label, half:, half:] += low
-        return carry
-
-    lax.fori_loop(0, (count + 1) // 2, add, 0)
+        return jnp.maximum(ready, needed)
+
+    ready = lax.fori_loop(0, (count + 1) // 2, add, 0)
+    lax.fori_loop(ready, groups, wait, 0)
     r = lax.broadcasted_iota(jnp.int32, (128, 128), 0)
     l = lax.broadcasted_iota(jnp.int32, (128, 128), 1)
     leaving = []
@@ -489,11 +500,13 @@
         out_specs=hbm,
         scratch_shapes=[
             pltpu.SMEM((3, 2 * arrived.shape[0] + 1), jnp.int32),
-            pltpu.VMEM((arrived.shape[0] + 1, *arrived.shape[1:]), F32),
+            pltpu.VMEM((arrived.shape[0], 8, 128), F32),
+            pltpu.VMEM((arrived.shape[0] + 1, 3 * width, 128), F32),
             pltpu.VMEM((slices, width, width), F32),
             pltpu.VMEM((slices, width, width), F32),
             pltpu.VMEM((2, slices, 128, 128), F32),
             pltpu.SemaphoreType.DMA((arrived.shape[0],)),
+            pltpu.SemaphoreType.DMA,
             pltpu.SemaphoreType.DMA,
             pltpu.SemaphoreType.DMA((width // 128,)),
         ],

time: 206 us -> 206 us (level); the launches traced: 204 us -> 207 us
  Pallas kernels: 77.6 us -> 80.5 us
    pallas_call x1, Pallas kernels: 25.7 us -> 28.6 us  [factor(): pl.pallas_call(factor_kernel, out_shape=jax.ShapeDtypeStruct(prior_gram.s...]
  transfers between devices with their start and end apart: 1 -> 1, of which waited for: 1 -> 1; matrix products, arithmetic and copies ran while one was open for 1% -> 1% of each run, Pallas kernels for 20% -> 19%
where the time goes in v1:
time: 206 us; the launch traced here: 207 us
  blocking collectives  82 us (40%)
  Pallas kernels  80.5 us (39%)
  waiting for transfers between devices  36.5 us (18%)
  starting transfers between devices  5.65 us (3%)
    all_to_all x1, blocking collectives, per_device(): lax.all_to_all(kept, 'arc', split_axis=0, concat_axis=0, tiled=True)  82 us
    pallas_call x1, Pallas kernels, local_part(): pl.pallas_call(local_kernel, out_shape=(jax.ShapeDtypeStruct((arcs, 2, ro...  39.8 us
    all_to_all x1, waiting for transfers between devices, per_device(): lax.all_to_all(packed, 'col', split_axis=0, concat_axis=0, tiled=True)  36.5 us
    pallas_call x1, Pallas kernels, factor(): pl.pallas_call(factor_kernel, out_shape=jax.ShapeDtypeStruct(prior_gram.s...  28.6 us
    pallas_call x1, Pallas kernels, eliminate(): pl.pallas_call(eliminate_kernel, out_shape=jax.ShapeDtypeStruct((groups,...  7.61 us
    all_to_all x1, starting transfers between devices, per_device(): lax.all_to_all(packed, 'col', split_axis=0, concat_axis=0, tiled=True)  5.65 us
    pallas_call x1, Pallas kernels, layout(): pl.pallas_call(layout_kernel, out_shape=jax.ShapeDtypeStruct((arcs, packe...  4.48 us
  transfers between devices with their start and end apart: 1, of which 1 were waited for; matrix products, arithmetic and copies ran while one was open for 1% of the time, Pallas kernels for 19%

profile of v1, /device:TPU:24, one launch (start us, length us, event | category | flops | bytes accessed | tf_op | source)
XLA Modules:
  0.0 206.6 jit_solution(11502427910542720837)
XLA Ops:
  0.0 4.5 %shard_map.55 = f32[128,80,128]{2,1,0:T(8,128)} custom-call(f32[320,32,128]{2,1,0:T(8,128)} %bitcast.2), custom_call_target="tpu_custom_call" | custom-call | tf_op jit(solution)/shard_map/pallas_call | solution.py:248
  4.5 0.0 copy-start.1
  4.5 0.0 copy-start.2
  4.5 5.6 %all-to-all-start = ((f32[128,80,128]{2,1,0:T(8,128)}), f32[128,80,128]{2,1,0:T(8,128)}, u32[]{:S(2)}, u32[]{:S(2)}) async-start(f32[128,80,128]{2,1,0:T(8,128)} %shard_map.55), calls=%async_computation | async-start | bytes 10485760 | tf_op jit(solution)/shard_map/all_to_all | solution.py:523
  10.2 0.0 copy-done.1
  10.2 0.6 dynamic_slice.3.counts_ref
  10.8 39.8 %shard_map.56 = (bf16[8,2,192,384]{3,2,1,0:T(8,128)(2,1)}, f32[2,512,512]{2,1,0:T(8,128)}) custom-call(s32[8]{0:T(128)} %dynamic_slice.3.counts_ref, f32[8,320,128]{2,1,0:T(8,128)} %l_ref.1, f32[2,512,512]{2,1,0:T(8,128)} %prior_ref.1), custom_call_target="tpu_custom_call" | custom-call | tf_op jit(solution)/shard_map/pallas_call | solution.py:309
  50.5 0.0 copy-done.2
  50.5 0.5 and_select_fusion
  51.1 0.0 copy-start
  51.1 0.7 convert_reduce_fusion.slot_ref
  51.8 36.5 %all-to-all-done = f32[128,80,128]{2,1,0:T(8,128)} async-done(((f32[128,80,128]{2,1,0:T(8,128)}), f32[128,80,128]{2,1,0:T(8,128)}, u32[]{:S(2)}, u32[]{:S(2)}) %all-to-all-start) | async-done | bytes 5242912 | tf_op jit(solution)/shard_map/all_to_all | solution.py:523
  88.2 0.0 copy-done
  88.2 7.6 %shard_map.57 = f32[8,1544,128]{2,1,0:T(8,128)} custom-call(s32[8]{0:T(128)} %copy-done, s32[8]{0:T(128)} %convert_reduce_fusion.slot_ref, s32[8]{0:T(128)} %get-tuple-element.9.label_ref, f32[16,8,80,128]{3,2,1,0:T(8,128)} %bitcast.1.g_hbm, bf16[8,2,192,384]{3,2,1,0:T(8,128)(2,1)} %get-tuple-element.7.z_hbm), custom_call_target="tpu_custom_call" | custom-call | tf_op jit(solution)/shard_map/pallas_call | solution.py:384
  95.9 82.0 %all_to_all.10.x_hbm = f32[8,1544,128]{2,1,0:T(8,128)} all-to-all(f32[8,1544,128]{2,1,0:T(8,128)} %shard_map.57), channel_id=1, replica_groups=mesh['arc'=8,'col'=16] {'arc'}, dimensions={0} | all-to-all | bytes 12648448 | tf_op jit(solution)/shard_map/all_to_all | solution.py:531
  177.9 28.6 %shard_map.58 = f32[2,512,512]{2,1,0:T(8,128)} custom-call(f32[8,1544,128]{2,1,0:T(8,128)} %all_to_all.10.x_hbm, f32[2,512,512]{2,1,0:T(8,128)} %get-tuple-element.8.prior_ref), custom_call_target="tpu_custom_call" | custom-call | tf_op jit(solution)/shard_map/pallas_call | solution.py:496
Async XLA Ops:
  4.5 5.7 %copy-start.1 = (s32[128]{0:T(128)S(1)}, s32[128]{0:T(128)}, u32[]{:S(2)}) copy-start(s32[128]{0:T(128)} %param.7) | copy-start | bytes 1540
  4.5 46.0 %copy-start.2 = (s32[8]{0:T(128)S(1)}, s32[8]{0:T(128)}, u32[]{:S(2)}) copy-start(s32[8]{0:T(128)} %param.8) | copy-start | bytes 100
  4.5 83.7 %all-to-all-start = ((f32[128,80,128]{2,1,0:T(8,128)}), f32[128,80,128]{2,1,0:T(8,128)}, u32[]{:S(2)}, u32[]{:S(2)}) async-start(f32[128,80,128]{2,1,0:T(8,128)} %shard_map.55), calls=%async_computation | async-start | bytes 10485760 | tf_op jit(solution)/shard_map/all_to_all | solution.py:523
  51.1 37.2 %copy-start = (s32[8]{0:T(128)}, s32[8]{0:T(128)S(1)}, u32[]{:S(2)}) copy-start(s32[8]{0:T(128)S(1)} %get-tuple-element.10.dest_ref) | copy-start | bytes 100
